TPU v7x, 512 devices: a whole 4x8x8 slice. The times are simulated.
512 devices in a mesh: pipe: 4 (over z_lo), expert: 64 (over y, x, core), dp: 2 (over z_hi).
Axes of the slice: x: 4, y: 8, z: 8 (z_hi: 2, z_lo: 4; z = z_hi * 4 + z_lo), core: 2. Of those that a mesh axis runs over, the one named last changes fastest.
Arguments:
- section_inputs: bfloat16 [4, 4096, 2048], P('pipe', ('expert', 'dp')), may hold values from -6 to 6
- saved_inputs: bfloat16 [4, 4096, 2048], P('pipe', ('expert', 'dp')), may hold values from -6 to 6
- output_grads: bfloat16 [4, 4096, 2048], P('pipe', ('expert', 'dp')), may hold values from -6 to 6
- forward_routes: int32 [4, 4096, 8], P('pipe', ('expert', 'dp')), may hold values from 0 to 63, as said below
- backward_routes: int32 [4, 4096, 8], P('pipe', ('expert', 'dp')), may hold values from 0 to 63, as said below
- forward_gates: float32 [4, 4096, 8], P('pipe', ('expert', 'dp')), may hold values from 0.1 to 0.9
- backward_gates: float32 [4, 4096, 8], P('pipe', ('expert', 'dp')), may hold values from 0.1 to 0.9
- expert_weights: bfloat16 [4, 64, 2048, 768], P('pipe', 'expert'), may hold values from -0.125 to 0.125
Outputs:
- next_inputs: bfloat16 [4, 4096, 2048], P('pipe', ('expert', 'dp'))
- prior_grads: bfloat16 [4, 4096, 2048], P('pipe', ('expert', 'dp'))
- weight_grads: bfloat16 [4, 64, 2048, 768], P('pipe', 'expert', 'dp')
Inputs may be any that keep to these rules, and one draw needn't show every extreme that they name: `forward_routes`: each token names 8 different experts. Among the tokens of one aligned block of 32 (the tokens of one device) no expert is named more than 5 times, and in each section one expert is named exactly 5 times in every block. `backward_routes`: as for forward_routes.
All inputs are finite; a program needn't handle non-finite values.
Results may differ from a plain program's by a relative error of at most 0.012.
Values may be sent and summed in bfloat16 or wider, within the bound.
A program may use at most 64 MiB of HBM per device.

v0:
```python
import functools

import jax
import jax.numpy as jnp
from jax import lax
from jax.experimental import pallas as pl
from jax.experimental.pallas import tpu as pltpu
from jax.sharding import PartitionSpec as P

MESH = pl.DeviceIdType.MESH
BF = jnp.bfloat16
F32 = jnp.float32
TOK = 32
CAP = 5
NY = 8
NQ = 8
WIDE = 1024
PAIRS = ((1, 7), (2, 6), (3, 5))
SLOT = NY * CAP
D = 2048
HID = 768
PIECES = 8
ORDER = (4, 5, 2, 3, 6, 7, 1)


def dot(a, b):
    return jnp.dot(a, b, preferred_element_type=F32)


def dot_t(a, b):
    return lax.dot_general(a, b, (((1,), (1,)), ((), ())), preferred_element_type=F32)


def dot_tl(a, b):
    return lax.dot_general(a, b, (((0,), (0,)), ((), ())), preferred_element_type=F32)


def tile(i, n):
    return pl.ds(pl.multiple_of(i * n, n), n)


def div(v, n):
    return lax.shift_right_logical(v * (-(-65536 // n)), 16)


def iota(shape, axis):
    return lax.broadcasted_iota(jnp.int32, shape, axis)


def kernel(
    rf_ref, rb_ref, gf_ref, gb_ref, s_hbm, o_hbm, f_hbm, w_hbm,
    next_ref, prior_ref, wg_ref,
    w, metas, xsg, xf, gsend, grecv, osend, orecv, first, fsend, frecv, rsend, rrecv, rows, pair, frow, fh,
    big, scale, undo, undo1, pack, comb, part, ysend, yrecv, out_send, out_recv, wsend, wrecv, wown,
    w_sem, in_sem, out_sem, ms, mr, gs, gr, xs, xr, bs, br, ys, yr, ds_, dr, ps, pr,
):
    e = lax.axis_index("expert")
    p = lax.axis_index("pipe")
    half = lax.axis_index("dp")
    y, q = e // NQ, e % NQ
    x, c = q // 2, q % 2

    def ydev(k):
        return {"expert": ((y + k + NY) % NY) * NQ + q}

    def qdev(j):
        jx, jc = j // 2, j % 2
        other = ((x // 2 + jx // 2) % 2) * 2 + (x % 2 + jx % 2) % 2
        return {"expert": y * NQ + other * 2 + (c + jc) % 2}

    def send(src, dst, ssem, rsem, dev):
        return pltpu.make_async_remote_copy(
            src_ref=src, dst_ref=dst, send_sem=ssem, recv_sem=rsem, device_id=dev, device_id_type=MESH
        )

    sent = []

    def start(copy):
        copy.start()
        sent.append(copy)
        return copy

    def arrive(copies):
        for copy in copies:
            copy.wait_recv()

    barrier = pltpu.get_barrier_semaphore()
    friends = [ydev(k) for k in range(1, NY)] + [qdev(j) for j in range(1, NQ)]
    friends += [{"dp": 1 - half}, {"pipe": (p + 1) % 4}, {"pipe": (p + 3) % 4}]
    for dev in friends:
        pl.semaphore_signal(barrier, inc=1, device_id=dev, device_id_type=MESH)

    inputs = [
        pltpu.make_async_copy(u, v, in_sem.at[i])
        for i, (u, v) in enumerate((
            (s_hbm, xsg.at[0, pl.ds(0, TOK)]),
            (o_hbm, xsg.at[0, pl.ds(TOK, TOK)]),
            (f_hbm.at[:, pl.ds(0, WIDE)], xf.at[0, pl.ds(0, TOK)]),
            (f_hbm.at[:, pl.ds(WIDE, WIDE)], xf.at[0, pl.ds(TOK, TOK)]),
        ))
    ]
    for copy in inputs:
        copy.start()
    w_copy = pltpu.make_async_copy(w_hbm, w, w_sem)
    w_copy.start()

    metas[0] = jnp.concatenate(
        [rf_ref[...].astype(F32), rb_ref[...].astype(F32), gf_ref[...], gb_ref[...]], axis=1
    )

    lane = div(iota((8, 128), 1), TOK)

    def lanes_of(kind, blocks):
        v = None
        for b, d in enumerate(blocks):
            shift = ((b - kind) * TOK) % 128
            u = metas[d]
            if shift:
                u = pltpu.roll(u, shift, 1)
            v = u if v is None else jnp.where(lane == b, u, v)
        return v

    expert = (y * NQ + jnp.bitwise_xor(iota((NQ, 128), 0), q)).astype(F32)

    def routed(t, blocks):
        routes, gates = lanes_of(t, blocks), lanes_of(2 + t, blocks)
        mark = jnp.zeros((NQ, 128), F32)
        gate = jnp.zeros((NQ, 128), F32)
        for k in range(8):
            same = routes[k : k + 1, :] == expert
            mark = mark + jnp.where(same, 1.0, 0.0)
            gate = gate + jnp.where(same, gates[k : k + 1, :], 0.0)
        return mark, gate

    r2, l2 = iota((128, 128), 0), iota((128, 128), 1)
    earlier = jnp.where((div(r2, TOK) == div(l2, TOK)) & (r2 < l2), 1.0, 0.0).astype(BF)

    def places_of(marks):
        return jnp.where(marks > 0.5, dot(marks.astype(BF), earlier), -1.0)

    spread = jnp.where(iota((640, NQ), 1) == div(iota((640, NQ), 0), 80), 1.0, 0.0)

    def prepare(n, spot, gate):
        r, l = iota((640, 128), 0), iota((640, 128), 1)
        r = r - div(r, 80) * 80
        l64 = div(l, 64)
        single = n in (0, 4)
        count = 10 if single else 20
        part_of = div(r, count)
        r = r - part_of * count
        tensor = div(r, count // 2)
        r = r - tensor * (count // 2)
        fits = div(l, TOK) - 2 * l64 == tensor
        if not single:
            b2 = div(r, CAP)
            fits = fits & (l64 == b2)
            r = r - b2 * CAP
        want = jnp.where(fits, r, -2).astype(F32)
        where = dot(spread.astype(BF), spot.astype(BF))
        hit = jnp.where(where == want, 1.0, 0.0)
        gate = jnp.dot(spread, gate, preferred_element_type=F32, precision=lax.Precision.HIGHEST)
        counted = jnp.where(l64 == 0, hit * gate, 0.0) if single else hit * gate
        total = jnp.sum(counted, axis=1, keepdims=True)
        scale[n] = jnp.where(tensor == 0, 1.0, jnp.broadcast_to(total, (640, 128)))
        for i in range(4):
            here = part_of == (2 * i + l64 if single else i)
            big[n, :, i * 128 : (i + 1) * 128] = jnp.where(here, hit, 0.0).astype(BF)

    def pack_single(n, d, k):
        stack = [xsg[d, :, i * 256 : (i + 1) * 256] for i in range(8)]
        v = dot(big[n], jnp.concatenate(stack, axis=0)) * scale[n, :, 0:1]
        v = v.astype(BF).reshape(NQ, 80, 256)
        orecv[k, 0] = v[0]
        osend[k, 1:] = v[1:]

    def send_single(n, k):
        return [start(send(osend.at[k, j], orecv.at[k, j], xs.at[n, j], xr.at[n, j], qdev(j))) for j in ORDER]

    mark, gate = routed(1, (0, 0, 0, 0))
    prepare(0, places_of(mark), gate)
    inputs[0].wait()
    inputs[1].wait()
    pack_single(0, 0, 0)

    pl.semaphore_wait(barrier, len(friends))

    def gather(i, step):
        buf = (xsg, xf)[i]
        copies = []
        for way in range(2):
            src, dst = ((NY - step + 1) % NY, NY - step) if way == 0 else (step - 1, step)
            if step < 4:
                a, b = buf.at[src], buf.at[dst]
            else:
                cut = pl.ds(way * TOK, TOK)
                a, b = buf.at[src, cut], buf.at[dst, cut]
            copies.append(start(send(a, b, gs.at[i, step - 1, way], gr.at[i, step - 1, way], ydev(1 - 2 * way))))
        return copies

    for k in (1, 7, 2, 6, 3, 5, 4):
        start(send(metas.at[0], metas.at[NY - k], ms.at[k], mr.at[NY - k], ydev(k)))
    g = {0: gather(0, 1)}

    gx = {0: send_single(0, 0)}
    inputs[2].wait()
    inputs[3].wait()

    def order(width):
        m, a = iota((640, 640), 1), iota((640, 640), 0)
        i = div(a, 8 * width)
        a = a - i * 8 * width
        tensor = div(a, 4 * width)
        a = a - tensor * 4 * width
        j = div(a, width // 2)
        a = a - j * (width // 2)
        return jnp.where(m == j * 80 + i * width + tensor * (width // 2) + a, 1.0, 0.0).astype(BF)

    undo[...] = order(20)

    for k in range(1, NY):
        send(metas.at[0], metas.at[k], ms.at[k], mr.at[k], ydev(k)).wait_recv()

    sets = [(1, (u, u, v, v)) for u, v in PAIRS] + [(1, (4, 4, 4, 4))]
    sets += [(t, tuple(range(4 * h, 4 * h + 4))) for t in range(2) for h in range(2)]
    found = [routed(*one) for one in sets]
    place = places_of(jnp.concatenate([one[0] for one in found], axis=0))
    places = [place[n * NQ : (n + 1) * NQ] for n in range(8)]
    gated = [one[1] for one in found]

    def dispatch(n):
        @pl.loop(0, 2)
        def _(h):
            stack = [
                xsg[d, :, pl.ds(pl.multiple_of(i * 512 + h * 256, 256), 256)]
                for i in range(4) for d in PAIRS[n - 1]
            ]
            v = dot(big[n], jnp.concatenate(stack, axis=0)) * scale[n, :, 0:1]
            v = v.astype(BF).reshape(NQ, 80, 256)
            grecv[n - 1, 0, :, tile(h, 256)] = v[0]
            gsend[n - 1, 1:, :, tile(h, 256)] = v[1:]

        return [
            start(send(gsend.at[n - 1, j], grecv.at[n - 1, j], xs.at[n, j], xr.at[n, j], qdev(j))) for j in ORDER
        ]

    def forward(step):
        arrive(g[1])
        g[1] = gather(1, step)

    wide = NY * TOK

    def full(v, t):
        return jnp.concatenate([v[4 + 2 * t], v[5 + 2 * t]], axis=1)

    zeros = jnp.zeros((SLOT, wide), F32)

    def slots(t):
        rr, ll = iota((SLOT, wide), 0), iota((SLOT, wide), 1)
        block = div(rr, CAP)
        d = block
        if t == 1:
            up = div(block, 2)
            d = jnp.where(block == 2 * up, up + 1, NY - 1 - up)
            d = jnp.where(block == 6, 0, jnp.where(block == 7, 4, d))
        target = jnp.where(div(ll, TOK) == d, rr - block * CAP, -2).astype(F32)
        ones, lefts, rights = [], [], []
        spot, gate = full(places, t), full(gated, t)
        for j in range(NQ):
            hit = jnp.where(spot[j : j + 1, :] == target, 1.0, 0.0)
            weight = hit * gate[j : j + 1, :] if t == 0 else hit
            ones.append(hit)
            lefts += [weight, zeros]
            rights += [zeros, weight]
        if t == 0:
            pack[...] = jnp.concatenate(ones, axis=0).astype(BF)
        comb[t, 0] = jnp.concatenate(lefts, axis=0).T.astype(BF)
        comb[t, 1] = jnp.concatenate(rights, axis=0).T.astype(BF)

    def hidden(n):
        @pl.loop(0, HID // 256)
        def _(k):
            v = dot(rows[n], w[:, tile(k, 256)])
            h, a = v[0:80], v[80:160]
            s = jax.nn.sigmoid(h)
            hg = a * s * (1.0 + h * (1.0 - s))
            pair[n, :, tile(k, 256)] = jnp.concatenate([hg, h * s], axis=0).astype(BF)

    def receive(n):
        arrive(gx[n])

        @pl.loop(0, 2)
        def _(h):
            v = dot(undo[...], grecv[n - 1, :, :, tile(h, 256)].reshape(640, 256)).astype(BF)
            for i in range(4):
                rows[n - 1, :, pl.ds(pl.multiple_of(i * 512 + h * 256, 256), 256)] = v[i * 160 : (i + 1) * 160]

        hidden(n - 1)

    for n in range(1, 5):
        prepare(n, places[n - 1], gated[n - 1])
        arrive(g[0])
        if n < 4:
            g[0] = gather(0, n + 1)
            if n == 3:
                g[1] = gather(1, 1)
            gx[n] = dispatch(n)
        else:
            pack_single(4, 4, 1)
            gx[4] = send_single(4, 1)
            forward(2)
        if n == 1:
            slots(0)
            undo1[...] = order(10)
            slots(1)
            w_copy.wait()
        elif n == 2:
            arrive(gx[0])
            first[...] = dot(undo1[...], orecv[0].reshape(640, 256))
            receive(1)
        else:
            receive(n - 1)

    forward(3)
    arrive(gx[4])
    last = dot(undo1[...], orecv[1].reshape(640, 256))
    for i in range(8):
        pieces = [v[i * 80 + h : i * 80 + h + 40] for h in (0, 40) for v in (first, last)]
        rows[3, :, i * 256 : (i + 1) * 256] = jnp.concatenate(pieces, axis=0).astype(BF)
    forward(4)
    hidden(3)

    per = WIDE // PIECES

    def weight_part(owner, k):
        at = pl.ds(pl.multiple_of(owner * WIDE + k * per, per), per)
        return dot_tl(rows[:, :, at].reshape(640, per), pair[...].reshape(640, HID)).astype(BF)

    wcopies = []

    def other_half(k):
        wsend[k] = weight_part(1 - half, k)
        wcopies.append(start(send(wsend.at[k], wrecv.at[k], ds_.at[k], dr.at[k], {"dp": 1 - half})))

    other_half(0)
    other_half(1)
    arrive(g[1])

    @pl.loop(0, WIDE // 256)
    def _(n):
        at = tile(n, 256)
        top = dot(pack[...], xf[:, 0:TOK, at].reshape(wide, 256))
        low = dot(pack[...], xf[:, TOK : 2 * TOK, at].reshape(wide, 256))
        for j in range(NQ):
            cut = slice(j * SLOT, (j + 1) * SLOT)
            msg = jnp.concatenate([top[cut], low[cut]], axis=0).astype(BF)
            if j == 0:
                frecv[0, :, at] = msg
            else:
                fsend[j, :, at] = msg

    fx = [start(send(fsend.at[j], frecv.at[j], xs.at[5, j], xr.at[5, j], qdev(j))) for j in ORDER]

    def give_back(t, source):
        copies = []
        for h in range(2):
            unit = 2 * t + h

            @pl.loop(0, 2)
            def _(n):
                at = tile(n, 256)
                left = dot_t(source, w[pl.ds(pl.multiple_of(h * 512 + n * 256, 256), 256), :])
                right = dot_t(source, w[pl.ds(pl.multiple_of(WIDE + h * 512 + n * 256, 256), 256), :])
                for j in range(NQ):
                    cut = slice(j * SLOT, (j + 1) * SLOT)
                    msg = jnp.concatenate([left[cut], right[cut]], axis=0).astype(BF)
                    if j == 0:
                        rrecv[unit, 0, :, at] = msg
                    else:
                        rsend[unit, j, :, at] = msg

            copies.append([
                start(send(rsend.at[unit, j], rrecv.at[unit, j], bs.at[unit, j], br.at[unit, j], qdev(j)))
                for j in ORDER
            ])
        return copies

    a = iota((320, 320), 0)
    j8 = div(a, 40)
    a = a - j8 * 40
    n4 = div(a, 10)
    a = a - n4 * 10
    b2 = div(a, CAP)
    source = jnp.where(n4 < 3, n4 * 80 + j8 * 10 + a, 240 + b2 * 40 + j8 * CAP + (a - b2 * CAP))
    turn = jnp.where(iota((320, 320), 1) == source, 1.0, 0.0).astype(BF)
    b1 = give_back(1, dot(turn, pair[:, 0:80, :].reshape(320, HID)).astype(BF))

    for k in range(2, PIECES):
        other_half(k)

    arrive(fx)

    @pl.loop(0, WIDE // 256)
    def _(n):
        v = frecv[:, :, tile(n, 256)].astype(F32)
        frow[:, tile(n, 256)] = v[:, 0:SLOT].reshape(SLOT * NQ, 256).astype(BF)
        frow[:, pl.ds(pl.multiple_of(WIDE + n * 256, 256), 256)] = v[:, SLOT:].reshape(SLOT * NQ, 256).astype(BF)

    @pl.loop(0, HID // 256)
    def _(n):
        h = dot(frow[...], w[:, tile(n, 256)])
        fh[:, tile(n, 256)] = (h * jax.nn.sigmoid(h)).astype(BF)

    b0 = give_back(0, fh[...])

    def combine(u):
        @pl.loop(0, 2)
        def _(n):
            at = tile(n, 256)
            got = rrecv[u, :, :, at].reshape(2 * SLOT * NQ, 256)
            part[u, :, 0:TOK, at] = dot(comb[u // 2, 0], got).reshape(NY, TOK, 256)
            part[u, :, TOK : 2 * TOK, at] = dot(comb[u // 2, 1], got).reshape(NY, TOK, 256)

    r = {}

    def reduce_step(u, step):
        copies = []
        for way in range(2):
            if step == 1:
                cut = slice(way * TOK, (way + 1) * TOK)
                ysend[u, 0, way, cut] = part[u, 4, cut].astype(BF)
                where = pl.ds(way * TOK, TOK)
                a, b = ysend.at[u, 0, way, where], yrecv.at[u, 0, way, where]
            else:
                s = step - 1
                r[u][way].wait_recv()
                d = 5 - step if way == 0 else 3 + step
                if step == 2:
                    got = slice(way * TOK, (way + 1) * TOK)
                    rest = slice((1 - way) * TOK, (2 - way) * TOK)
                    ysend[u, s, way, got] = (part[u, d, got] + yrecv[u, 0, way, got].astype(F32)).astype(BF)
                    ysend[u, s, way, rest] = part[u, d, rest].astype(BF)
                else:
                    ysend[u, s, way] = (part[u, d] + yrecv[u, s - 1, way].astype(F32)).astype(BF)
                a, b = ysend.at[u, s, way], yrecv.at[u, s, way]
            copies.append(start(send(a, b, ys.at[u, step - 1, way], yr.at[u, step - 1, way], ydev(1 - 2 * way))))
        r[u] = copies

    pipes = {}

    def finish(u):
        arrive(r[u])
        total = part[u, 0] + yrecv[u, 3, 0].astype(F32) + yrecv[u, 3, 1].astype(F32)
        t, h = u // 2, u % 2
        for i in range(2):
            if t == 1:
                base = xsg[0, TOK : 2 * TOK, i * WIDE + h * 512 : i * WIDE + h * 512 + 512]
            else:
                base = xf[0, i * TOK : (i + 1) * TOK, h * 512 : h * 512 + 512]
            cut = slice(i * TOK, (i + 1) * TOK)
            out_send[u, cut] = (base.astype(F32) + total[cut]).astype(BF)
        to = (p + (3 if t == 1 else 1)) % 4
        pipes[u] = start(send(out_send.at[u], out_recv.at[u], ps.at[u], pr.at[u], {"pipe": to}))

    def own_half(k):
        wown[k] = weight_part(half, k)

    outs = []

    def place_out(src, dst):
        copy = pltpu.make_async_copy(src, dst, out_sem.at[len(outs)])
        copy.start()
        outs.append(copy)

    def sum_half(k):
        wcopies[k].wait_recv()
        wown[k] = (wown[k].astype(F32) + wrecv[k].astype(F32)).astype(BF)
        place_out(wown.at[k], wg_ref.at[pl.ds(k * per, per)])

    waits = {2: b1[0], 3: b1[1], 0: b0[0], 1: b0[1]}
    begun = {2: 0, 3: 2, 0: 4, 1: 6}
    pieces = list(range(PIECES))
    for tick in range(11):
        for u in (2, 3, 0, 1):
            step = tick - begun[u] + 1
            if step == 1:
                arrive(waits[u])
                combine(u)
            if 1 <= step <= 4:
                reduce_step(u, step)
            if step == 5:
                finish(u)
        for _ in range(2):
            if pieces:
                own_half(pieces.pop(0))
        if tick in (4, 6, 8, 9):
            sum_half((4, 6, 8, 9).index(tick))

    def take(u):
        pipes[u].wait_recv()
        out = prior_ref if u >= 2 else next_ref
        for i in range(2):
            place_out(out_recv.at[u, pl.ds(i * TOK, TOK)], out.at[:, pl.ds(i * WIDE + (u % 2) * 512, 512)])

    take(2)
    take(3)
    for k in range(4, PIECES):
        sum_half(k)
    take(0)
    take(1)
    for copy in outs:
        copy.wait()
    for copy in sent:
        copy.wait_send()


def finish_kernel(a, b, c, x, y, z, va, vb, vc, sems):
    pieces = [(c.at[pl.ds(i * 256, 256)], vc.at[i], z.at[pl.ds(i * 256, 256)]) for i in range(4)]
    pieces += [(a, va, x), (b, vb, y)]
    loads = [pltpu.make_async_copy(u, m, sems.at[0, i]) for i, (u, m, _) in enumerate(pieces)]
    stores = [pltpu.make_async_copy(m, o, sems.at[1, i]) for i, (_, m, o) in enumerate(pieces)]
    for copy in loads:
        copy.start()
    for load, store in zip(loads, stores):
        load.wait()
        store.start()
    for copy in stores:
        copy.wait()


def relay(rf, rb, gf, gb, s, o, f, w):
    vmem = pl.BlockSpec(memory_space=pltpu.VMEM)
    dma = pltpu.SemaphoreType.DMA
    v = pltpu.VMEM
    two = 2 * SLOT
    return pl.pallas_call(
        kernel,
        out_shape=(
            jax.ShapeDtypeStruct((TOK, D), BF),
            jax.ShapeDtypeStruct((TOK, D), BF),
            jax.ShapeDtypeStruct((D // 2, HID), BF),
        ),
        in_specs=[vmem] * 4 + [pl.BlockSpec(memory_space=pl.ANY)] * 4,
        out_specs=(pl.BlockSpec(memory_space=pl.ANY),) * 3,
        scratch_shapes=[
            v((D, HID), BF),
            v((NY, 8, 128), F32),
            v((NY, 2 * TOK, D), BF),
            v((NY, 2 * TOK, WIDE), BF),
            v((3, NQ, two, 512), BF),
            v((3, NQ, two, 512), BF),
            v((2, NQ, two, 256), BF),
            v((2, NQ, two, 256), BF),
            v((640, 256), F32),
            v((NQ, two, WIDE), BF),
            v((NQ, two, WIDE), BF),
            v((4, NQ, two, 512), BF),
            v((4, NQ, two, 512), BF),
            v((4, 160, D), BF),
            v((4, 160, HID), BF),
            v((SLOT * NQ, D), BF),
            v((SLOT * NQ, HID), BF),
            v((5, 640, 512), BF),
            v((5, 640, 128), F32),
            v((640, 640), BF),
            v((640, 640), BF),
            v((SLOT * NQ, NY * TOK), BF),
            v((2, 2, NY * TOK, two * NQ), BF),
            v((4, NY, 2 * TOK, 512), F32),
            v((4, 4, 2, 2 * TOK, 512), BF),
            v((4, 4, 2, 2 * TOK, 512), BF),
            v((4, 2 * TOK, 512), BF),
            v((4, 2 * TOK, 512), BF),
            v((PIECES, WIDE // PIECES, HID), BF),
            v((PIECES, WIDE // PIECES, HID), BF),
            v((PIECES, WIDE // PIECES, HID), BF),
            dma,
            dma((4,)),
            dma((PIECES + 8,)),
            dma((NY,)), dma((NY,)),
            dma((2, 4, 2)), dma((2, 4, 2)),
            dma((6, NQ)), dma((6, NQ)),
            dma((4, NQ)), dma((4, NQ)),
            dma((4, 4, 2)), dma((4, 4, 2)),
            dma((PIECES,)), dma((PIECES,)),
            dma((4,)), dma((4,)),
        ],
        compiler_params=pltpu.CompilerParams(
            collective_id=0, has_side_effects=True, vmem_limit_bytes=58 << 20
        ),
        cost_estimate=pl.CostEstimate(flops=8 * 10**9, bytes_accessed=10**7, transcendentals=10**6),
        name="relay",
    )(rf, rb, gf, gb, s, o, f, w)


def on_device(section_inputs, saved_inputs, output_grads, forward_routes, backward_routes,
              forward_gates, backward_gates, expert_weights):
    outs = relay(
        forward_routes[0].T, backward_routes[0].T, forward_gates[0].T, backward_gates[0].T,
        saved_inputs[0], output_grads[0], section_inputs[0], expert_weights[0, 0],
    )
    anywhere = pl.BlockSpec(memory_space=pl.ANY)
    after, prior, wg = pl.pallas_call(
        finish_kernel,
        out_shape=[jax.ShapeDtypeStruct(v.shape, v.dtype) for v in outs],
        in_specs=[anywhere] * 3,
        out_specs=[anywhere] * 3,
        scratch_shapes=[
            pltpu.VMEM((TOK, D), BF),
            pltpu.VMEM((TOK, D), BF),
            pltpu.VMEM((4, 256, HID), BF),
            pltpu.SemaphoreType.DMA((2, 6)),
        ],
        name="place",
    )(*outs)
    return after[None], prior[None], wg[None, None]


def solution(mesh):
    placed = P("pipe", ("expert", "dp"), None)
    return jax.shard_map(
        on_device,
        mesh=mesh,
        in_specs=(placed,) * 7 + (P("pipe", "expert", None, None),),
        out_specs=(placed, placed, P("pipe", "expert", "dp", None)),
        check_vma=False,
    )
```

profile of v0, /device:TPU:1, one launch (start us, length us, event | category | flops | bytes accessed | tf_op | source)
XLA Modules:
  0.0 139.1 jit_solution(657512893748140329)
XLA Ops:
  0.6 136.0 %relay.1 = (bf16[32,2048]{1,0:T(8,128)(2,1)}, bf16[32,2048]{1,0:T(8,128)(2,1)}, bf16[1024,768]{1,0:T(8,128)(2,1)}) custom-call(s32[8,32]{1,0:T(8,128)} %bitcast.26, s32[8,32]{1,0:T(8,128)} %bitcast.27, f32[8,32]{1,0:T(8,128)} %bitcast.28, f32[8,32]{1,0:T(8,128)} %bitcast.29, bf16[32,2048]{1,0:T(8,128)(2,1)} %bitcast.21, bf16[32,2048]{1,0:T(8,128)(2,1)} %bitcast.22, ...), custom_call_target="tpu_custom_call" | custom-call | flops 8000000000 | bytes 10000000 | tf_op jit(solution)/shard_map/relay/pallas_call | solution.py:535
  136.6 2.3 %place.1 = (bf16[32,2048]{1,0:T(8,128)(2,1)}, bf16[32,2048]{1,0:T(8,128)(2,1)}, bf16[1024,768]{1,0:T(8,128)(2,1)}) custom-call(bf16[32,2048]{1,0:T(8,128)(2,1)} %get-tuple-element.9.a, bf16[32,2048]{1,0:T(8,128)(2,1)} %get-tuple-element.10.b, bf16[1024,768]{1,0:T(8,128)(2,1)} %get-tuple-element.11.c), custom_call_target="tpu_custom_call" | custom-call | tf_op jit(solution)/shard_map/place/pallas_call | solution.py:602
where the time goes:
time: 139 us
  Pallas kernels  138 us (99%)
    pallas_call x1, Pallas kernels, relay(): pl.pallas_call(kernel, out_shape=(jax.ShapeDtypeStruct((TOK, D), BF), jax...  136 us

commit v1 on v0

--- a/solution.py
+++ b/solution.py
@@ -204,6 +204,7 @@
     gx = {0: send_single(0, 0)}
     inputs[2].wait()
     inputs[3].wait()
+    g[1] = gather(1, 1)
 
     def order(width):
         m, a = iota((640, 640), 1), iota((640, 640), 0)
@@ -296,18 +297,34 @@
 
         hidden(n - 1)
 
+    def forward_rows():
+        @pl.loop(0, WIDE // 256)
+        def _(n):
+            at = tile(n, 256)
+            top = dot(pack[...], xf[:, 0:TOK, at].reshape(wide, 256))
+            low = dot(pack[...], xf[:, TOK : 2 * TOK, at].reshape(wide, 256))
+            for j in range(NQ):
+                cut = slice(j * SLOT, (j + 1) * SLOT)
+                msg = jnp.concatenate([top[cut], low[cut]], axis=0).astype(BF)
+                if j == 0:
+                    frecv[0, :, at] = msg
+                else:
+                    fsend[j, :, at] = msg
+
+        return [start(send(fsend.at[j], frecv.at[j], xs.at[5, j], xr.at[5, j], qdev(j))) for j in ORDER]
+
     for n in range(1, 5):
         prepare(n, places[n - 1], gated[n - 1])
         arrive(g[0])
         if n < 4:
             g[0] = gather(0, n + 1)
-            if n == 3:
-                g[1] = gather(1, 1)
             gx[n] = dispatch(n)
+            forward(n + 1)
         else:
             pack_single(4, 4, 1)
             gx[4] = send_single(4, 1)
-            forward(2)
+            arrive(g[1])
+            fx = forward_rows()
         if n == 1:
             slots(0)
             undo1[...] = order(10)
@@ -320,13 +337,11 @@
         else:
             receive(n - 1)
 
-    forward(3)
     arrive(gx[4])
     last = dot(undo1[...], orecv[1].reshape(640, 256))
     for i in range(8):
         pieces = [v[i * 80 + h : i * 80 + h + 40] for h in (0, 40) for v in (first, last)]
         rows[3, :, i * 256 : (i + 1) * 256] = jnp.concatenate(pieces, axis=0).astype(BF)
-    forward(4)
     hidden(3)
 
     per = WIDE // PIECES
@@ -342,24 +357,6 @@
         wcopies.append(start(send(wsend.at[k], wrecv.at[k], ds_.at[k], dr.at[k], {"dp": 1 - half})))
 
     other_half(0)
-    other_half(1)
-    arrive(g[1])
-
-    @pl.loop(0, WIDE // 256)
-    def _(n):
-        at = tile(n, 256)
-        top = dot(pack[...], xf[:, 0:TOK, at].reshape(wide, 256))
-        low = dot(pack[...], xf[:, TOK : 2 * TOK, at].reshape(wide, 256))
-        for j in range(NQ):
-            cut = slice(j * SLOT, (j + 1) * SLOT)
-            msg = jnp.concatenate([top[cut], low[cut]], axis=0).astype(BF)
-            if j == 0:
-                frecv[0, :, at] = msg
-            else:
-                fsend[j, :, at] = msg
-
-    fx = [start(send(fsend.at[j], frecv.at[j], xs.at[5, j], xr.at[5, j], qdev(j))) for j in ORDER]
-
     def give_back(t, source):
         copies = []
         for h in range(2):
@@ -394,7 +391,7 @@
     turn = jnp.where(iota((320, 320), 1) == source, 1.0, 0.0).astype(BF)
     b1 = give_back(1, dot(turn, pair[:, 0:80, :].reshape(320, HID)).astype(BF))
 
-    for k in range(2, PIECES):
+    for k in range(1, 4):
         other_half(k)
 
     arrive(fx)
@@ -411,6 +408,8 @@
         fh[:, tile(n, 256)] = (h * jax.nn.sigmoid(h)).astype(BF)
 
     b0 = give_back(0, fh[...])
+    for k in range(4, PIECES):
+        other_half(k)
 
     def combine(u):
         @pl.loop(0, 2)

time: 139 us -> 142 us (1.022)
  Pallas kernels: 138 us -> 141 us
    pallas_call x1, Pallas kernels: 136 us -> 138 us  [relay(): pl.pallas_call(kernel, out_shape=(jax.ShapeDtypeStruct((TOK, D), BF), jax...]
where the time goes in v1:
time: 142 us; the launch traced here: 141 us
  Pallas kernels  141 us (99%)
    pallas_call x1, Pallas kernels, relay(): pl.pallas_call(kernel, out_shape=(jax.ShapeDtypeStruct((TOK, D), BF), jax...  138 us

profile of v1, /device:TPU:1, one launch (start us, length us, event | category | flops | bytes accessed | tf_op | source)
XLA Modules:
  0.0 141.3 jit_solution(14691429492078402494)
XLA Ops:
  0.6 138.2 %relay.1 = (bf16[32,2048]{1,0:T(8,128)(2,1)}, bf16[32,2048]{1,0:T(8,128)(2,1)}, bf16[1024,768]{1,0:T(8,128)(2,1)}) custom-call(s32[8,32]{1,0:T(8,128)} %bitcast.26, s32[8,32]{1,0:T(8,128)} %bitcast.27, f32[8,32]{1,0:T(8,128)} %bitcast.28, f32[8,32]{1,0:T(8,128)} %bitcast.29, bf16[32,2048]{1,0:T(8,128)(2,1)} %bitcast.21, bf16[32,2048]{1,0:T(8,128)(2,1)} %bitcast.22, ...), custom_call_target="tpu_custom_call" | custom-call | flops 8000000000 | bytes 10000000 | tf_op jit(solution)/shard_map/relay/pallas_call | solution.py:534
  138.8 2.3 %place.1 = (bf16[32,2048]{1,0:T(8,128)(2,1)}, bf16[32,2048]{1,0:T(8,128)(2,1)}, bf16[1024,768]{1,0:T(8,128)(2,1)}) custom-call(bf16[32,2048]{1,0:T(8,128)(2,1)} %get-tuple-element.9.a, bf16[32,2048]{1,0:T(8,128)(2,1)} %get-tuple-element.10.b, bf16[1024,768]{1,0:T(8,128)(2,1)} %get-tuple-element.11.c), custom_call_target="tpu_custom_call" | custom-call | tf_op jit(solution)/shard_map/place/pallas_call | solution.py:601

commit v2 on v1

--- a/solution.py
+++ b/solution.py
@@ -323,8 +323,6 @@
         else:
             pack_single(4, 4, 1)
             gx[4] = send_single(4, 1)
-            arrive(g[1])
-            fx = forward_rows()
         if n == 1:
             slots(0)
             undo1[...] = order(10)
@@ -357,6 +355,8 @@
         wcopies.append(start(send(wsend.at[k], wrecv.at[k], ds_.at[k], dr.at[k], {"dp": 1 - half})))
 
     other_half(0)
+    arrive(g[1])
+    fx = forward_rows()
     def give_back(t, source):
         copies = []
         for h in range(2):
@@ -391,7 +391,7 @@
     turn = jnp.where(iota((320, 320), 1) == source, 1.0, 0.0).astype(BF)
     b1 = give_back(1, dot(turn, pair[:, 0:80, :].reshape(320, HID)).astype(BF))
 
-    for k in range(1, 4):
+    for k in range(1, 3):
         other_half(k)
 
     arrive(fx)
@@ -408,7 +408,7 @@
         fh[:, tile(n, 256)] = (h * jax.nn.sigmoid(h)).astype(BF)
 
     b0 = give_back(0, fh[...])
-    for k in range(4, PIECES):
+    for k in range(3, 4):
         other_half(k)
 
     def combine(u):
@@ -478,6 +478,7 @@
     waits = {2: b1[0], 3: b1[1], 0: b0[0], 1: b0[1]}
     begun = {2: 0, 3: 2, 0: 4, 1: 6}
     pieces = list(range(PIECES))
+    later = (1, 3, 5, 7)
     for tick in range(11):
         for u in (2, 3, 0, 1):
             step = tick - begun[u] + 1
@@ -491,6 +492,8 @@
         for _ in range(2):
             if pieces:
                 own_half(pieces.pop(0))
+        if tick in later:
+            other_half(4 + later.index(tick))
         if tick in (4, 6, 8, 9):
             sum_half((4, 6, 8, 9).index(tick))
 

time: 142 us -> 139 us (0.979)
  Pallas kernels: 141 us -> 138 us
    pallas_call x1, Pallas kernels: 138 us -> 136 us  [relay(): pl.pallas_call(kernel, out_shape=(jax.ShapeDtypeStruct((TOK, D), BF), jax...]
where the time goes in v2:
time: 139 us
  Pallas kernels  138 us (99%)
    pallas_call x1, Pallas kernels, relay(): pl.pallas_call(kernel, out_shape=(jax.ShapeDtypeStruct((TOK, D), BF), jax...  136 us

profile of v2, /device:TPU:1, one launch (start us, length us, event | category | flops | bytes accessed | tf_op | source)
XLA Modules:
  0.0 138.9 jit_solution(13394360589029448087)
XLA Ops:
  0.6 135.8 %relay.1 = (bf16[32,2048]{1,0:T(8,128)(2,1)}, bf16[32,2048]{1,0:T(8,128)(2,1)}, bf16[1024,768]{1,0:T(8,128)(2,1)}) custom-call(s32[8,32]{1,0:T(8,128)} %bitcast.26, s32[8,32]{1,0:T(8,128)} %bitcast.27, f32[8,32]{1,0:T(8,128)} %bitcast.28, f32[8,32]{1,0:T(8,128)} %bitcast.29, bf16[32,2048]{1,0:T(8,128)(2,1)} %bitcast.21, bf16[32,2048]{1,0:T(8,128)(2,1)} %bitcast.22, ...), custom_call_target="tpu_custom_call" | custom-call | flops 8000000000 | bytes 10000000 | tf_op jit(solution)/shard_map/relay/pallas_call | solution.py:537
  136.4 2.3 %place.1 = (bf16[32,2048]{1,0:T(8,128)(2,1)}, bf16[32,2048]{1,0:T(8,128)(2,1)}, bf16[1024,768]{1,0:T(8,128)(2,1)}) custom-call(bf16[32,2048]{1,0:T(8,128)(2,1)} %get-tuple-element.9.a, bf16[32,2048]{1,0:T(8,128)(2,1)} %get-tuple-element.10.b, bf16[1024,768]{1,0:T(8,128)(2,1)} %get-tuple-element.11.c), custom_call_target="tpu_custom_call" | custom-call | tf_op jit(solution)/shard_map/place/pallas_call | solution.py:604

commit v3 on v2

--- a/solution.py
+++ b/solution.py
@@ -335,6 +335,8 @@
         else:
             receive(n - 1)
 
+    arrive(g[1])
+    fx = forward_rows()
     arrive(gx[4])
     last = dot(undo1[...], orecv[1].reshape(640, 256))
     for i in range(8):
@@ -355,8 +357,6 @@
         wcopies.append(start(send(wsend.at[k], wrecv.at[k], ds_.at[k], dr.at[k], {"dp": 1 - half})))
 
     other_half(0)
-    arrive(g[1])
-    fx = forward_rows()
     def give_back(t, source):
         copies = []
         for h in range(2):

time: 139 us -> 139 us (level)
  no operation moved by 1% of the time
where the time goes in v3:
time: 139 us
  Pallas kernels  138 us (99%)
    pallas_call x1, Pallas kernels, relay(): pl.pallas_call(kernel, out_shape=(jax.ShapeDtypeStruct((TOK, D), BF), jax...  136 us

profile of v3, /device:TPU:1, one launch (start us, length us, event | category | flops | bytes accessed | tf_op | source)
XLA Modules:
  0.0 138.8 jit_solution(6451273088796299962)
XLA Ops:
  0.6 135.6 %relay.1 = (bf16[32,2048]{1,0:T(8,128)(2,1)}, bf16[32,2048]{1,0:T(8,128)(2,1)}, bf16[1024,768]{1,0:T(8,128)(2,1)}) custom-call(s32[8,32]{1,0:T(8,128)} %bitcast.26, s32[8,32]{1,0:T(8,128)} %bitcast.27, f32[8,32]{1,0:T(8,128)} %bitcast.28, f32[8,32]{1,0:T(8,128)} %bitcast.29, bf16[32,2048]{1,0:T(8,128)(2,1)} %bitcast.21, bf16[32,2048]{1,0:T(8,128)(2,1)} %bitcast.22, ...), custom_call_target="tpu_custom_call" | custom-call | flops 8000000000 | bytes 10000000 | tf_op jit(solution)/shard_map/relay/pallas_call | solution.py:537
  136.3 2.3 %place.1 = (bf16[32,2048]{1,0:T(8,128)(2,1)}, bf16[32,2048]{1,0:T(8,128)(2,1)}, bf16[1024,768]{1,0:T(8,128)(2,1)}) custom-call(bf16[32,2048]{1,0:T(8,128)(2,1)} %get-tuple-element.9.a, bf16[32,2048]{1,0:T(8,128)(2,1)} %get-tuple-element.10.b, bf16[1024,768]{1,0:T(8,128)(2,1)} %get-tuple-element.11.c), custom_call_target="tpu_custom_call" | custom-call | tf_op jit(solution)/shard_map/place/pallas_call | solution.py:604
